TPU v7x, 32 devices: a whole 2x2x4 slice. The times are simulated.
32 devices in a mesh: groups: 2 (over x), tm: 8 (over z, y), band: 2 (over core).
Axes of the slice: x: 2, y: 2, z: 4, core: 2. Of those that a mesh axis runs over, the one named last changes fastest.
Arguments:
- series: float32 [262144], P(('groups', 'tm')), parts along dimension 0, may hold values from -40 to 40
- tail: float32 [512], P('groups'), parts along dimension 0, may hold values from -6 to 6
- band_starts: int32 [4], P('groups'), parts along dimension 0, may hold values from 0 to 3968, as said below
Outputs:
- row_profile: float32 [262144], P(('groups', 'tm')), parts along dimension 0
- col_profile: float32 [262144], P(('groups', 'tm')), parts along dimension 0
There are 2 independent parts, one for each index of `groups`. A program takes and returns all parts, laid end to end along the dimension named above; each array names one. Nothing has to cross between parts.
Inputs may be any that keep to these rules, and one draw needn't show every extreme that they name: `band_starts`: one entry equals 3968.
All inputs are finite; a program needn't handle non-finite values.
Results may differ from a plain program's by a relative error of at most 0.00061.
Values sent between devices are 32-bit elements; how exact they have to be, the bound alone decides.
A program may use at most 64 MiB of HBM per device.

v0:
```python
import jax
import jax.numpy as jnp
from jax import lax
from jax.sharding import PartitionSpec as P

M = 256
TILE = 128
OFF_DEV = 128
BAND_SPAN = 4096
BAND_BLOCKS = 4


EPS = 1e-06
tile_batch = 16


def from_behind(block, axis, distance):
    devices = range(lax.axis_size(axis))
    route = [(i - distance, i) for i in devices if i - distance in devices]
    return lax.ppermute(block, axis, route)


def hankel(samples, tile_count):
    length = tile_count * TILE + M
    shifted = jnp.stack(
        [lax.slice_in_dim(samples, offset, offset + length) for offset in range(TILE)]
    )
    blocks = shifted.reshape(TILE, length // TILE, TILE)
    joined = jnp.concatenate(
        [blocks[:, stride : stride + tile_count] for stride in range(M // TILE)], axis=2
    )
    return jnp.swapaxes(joined, 0, 1)


def moments(matrix):
    center = jnp.mean(matrix, axis=-1)
    spread = matrix - center[..., None]
    factor = lax.rsqrt(jnp.sum(spread * spread, axis=-1) + M * EPS)
    return (center, factor)


def normed(matrix, center, factor):
    return ((matrix - center[..., None]) * factor[..., None]).astype(jnp.bfloat16)


def score_group(row_z, col_z, room_left):
    tile_count = row_z.shape[0]
    near_scores = jnp.einsum("tim,tjm->tij", row_z, col_z[:-1], preferred_element_type=jnp.float32)
    far_scores = jnp.einsum(
        "tim,tjm->tij", row_z, col_z[1:, :OFF_DEV], preferred_element_type=jnp.float32
    )
    row_near = lax.broadcasted_iota(jnp.int32, (TILE, TILE), 0)
    col_near = lax.broadcasted_iota(jnp.int32, (TILE, TILE), 1)
    row_far = lax.broadcasted_iota(jnp.int32, (TILE, OFF_DEV), 0)
    col_far = lax.broadcasted_iota(jnp.int32, (TILE, OFF_DEV), 1)
    tile_index = jnp.arange(tile_count, dtype=jnp.int32)[:, None, None]
    keep_near = (
        (col_near >= row_near)[None]
        & (col_near - row_near < OFF_DEV)[None]
        & (tile_index * TILE + col_near[None] < room_left)
    )
    keep_far = (TILE + col_far - row_far < OFF_DEV)[None] & (
        (tile_index + 1) * TILE + col_far[None] < room_left
    )
    near_scores = jnp.where(keep_near, near_scores, -1.0)
    far_scores = jnp.where(keep_far, far_scores, -1.0)
    best_rows = jnp.maximum(near_scores.max(axis=2), far_scores.max(axis=2)).reshape(-1)
    floor_row = jnp.full((1, TILE), -1.0, jnp.float32)
    upper_part = jnp.concatenate([near_scores.max(axis=1), floor_row], axis=0)
    far_cols = far_scores.max(axis=1)
    lower_part = jnp.concatenate([floor_row, far_cols], axis=0)
    return (best_rows, jnp.maximum(upper_part, lower_part).reshape(-1))


def place_columns(col_groups, start, buffer_len):
    group_rows = tile_batch * TILE
    count = col_groups.shape[0]
    main_part = col_groups[:, :group_rows].reshape(-1)
    carry_part = jnp.concatenate(
        [col_groups[:, group_rows:], jnp.full((count, group_rows - TILE), -1.0, jnp.float32)],
        axis=1,
    ).reshape(-1)
    shifted = jnp.concatenate([jnp.full((group_rows,), -1.0, jnp.float32), carry_part])[
        : count * group_rows + TILE
    ]
    reached = jnp.maximum(
        jnp.concatenate([main_part, jnp.full((TILE,), -1.0, jnp.float32)]), shifted
    )
    buffer_all = jnp.full((buffer_len,), -1.0, jnp.float32)
    return lax.dynamic_update_slice(buffer_all, reached, (start,))


def body(series, tail, band_starts):
    block_len = series.shape[0]
    group_rows = tile_batch * TILE
    group_count = block_len // group_rows
    position = lax.axis_index("tm")
    devices = lax.axis_size("tm")
    distance = BAND_BLOCKS
    following = from_behind(series[:M], "tm", -1)
    following = jnp.where(position == devices - 1, tail, following)
    extended = jnp.concatenate([series, following])
    row_source = jnp.concatenate([extended, jnp.zeros((TILE,), jnp.float32)])

    def own_group(group_index):
        row_piece = lax.dynamic_slice_in_dim(
            row_source, group_index * group_rows, group_rows + M + TILE
        )
        matrix = hankel(row_piece, tile_batch)
        center, factor = moments(matrix)
        return (center.reshape(-1), factor.reshape(-1), normed(matrix, center, factor))

    centers, factors, row_z = lax.map(own_group, jnp.arange(group_count, dtype=jnp.int32))
    centers = centers.reshape(block_len)
    factors = factors.reshape(block_len)
    padding = jnp.zeros((2 * TILE,), jnp.float32)
    far_samples = from_behind(extended, "tm", -distance)
    next_samples = from_behind(series[M : M + BAND_SPAN], "tm", -distance - 1)
    pair_samples = jnp.concatenate([far_samples, next_samples, padding])
    buffer_len = block_len + BAND_SPAN + TILE
    band_count = band_starts.shape[0]
    band_here = lax.axis_index("band")
    offset_start = jnp.sum(
        jnp.where(jnp.arange(band_count, dtype=jnp.int32) == band_here, band_starts, 0)
    )
    room_all = (devices - position - distance) * block_len - offset_start

    def pair_group(inputs):
        group_index, group_z = inputs
        col_begin = offset_start + group_index * group_rows
        col_piece = lax.dynamic_slice_in_dim(pair_samples, col_begin, (tile_batch + 2) * TILE + M)
        matrix = hankel(col_piece, tile_batch + 1)
        center, factor = moments(matrix)
        col_z = normed(matrix, center, factor)
        return score_group(group_z, col_z, room_all - group_index * group_rows)

    row_best, col_groups = lax.map(pair_group, (jnp.arange(group_count, dtype=jnp.int32), row_z))
    lifted = place_columns(col_groups, offset_start, buffer_len) + 1.0
    returned = from_behind(lifted[:block_len], "tm", distance)
    returned_head = from_behind(lifted[block_len : block_len + BAND_SPAN], "tm", distance + 1)
    col_best = (
        jnp.maximum(
            returned,
            jnp.concatenate([returned_head, jnp.zeros((block_len - BAND_SPAN,), jnp.float32)]),
        )
        - 1.0
    )
    return lax.pmax((row_best.reshape(block_len), col_best), "band")


def solution(mesh):
    placed = (P(("groups", "tm")), P("groups"), P("groups"))
    return jax.shard_map(
        body,
        mesh=mesh,
        in_specs=placed,
        out_specs=(P(("groups", "tm")), P(("groups", "tm"))),
        check_vma=False,
    )
```

profile of v0, /device:TPU:0, one launch (start us, length us, event | category | flops | bytes accessed | tf_op | source)
XLA Modules:
  0.0 258.0 jit_solution(17641519265853953807)
XLA Ops:
  18.1 81.0 %while.22 = (s32[]{:T(128)}, bf16[8,16,128,256]{3,2,1,0:T(8,128)(2,1)}, s32[8]{0:T(128)S(1)}, f32[16768]{0:T(1024)S(1)}, s32[]{:T(128)}, /*index=5*/s32[1]{0:T(1...) while((s32[]{:T(128)}, ...), condition=%wide.region_3.4_spmd, body=%wide.region_0.3_spmd.sunk | while | flops 5243013 | bytes 18689660 | solution.py:113
  23.6 1.9 stack.1160
  33.7 1.9 stack.1160
  43.8 1.9 stack.1160
  53.9 1.9 stack.1160
  64.0 1.9 stack.1160
  74.2 1.9 stack.1160
  84.3 1.9 stack.1160
  94.4 1.9 stack.1160
  99.2 114.6 %while.23 = (s32[]{:T(128)}, f32[8,2048]{1,0:T(8,128)S(1)}, f32[8,2176]{1,0:T(8,128)S(1)}, s32[8]{0:T(128)S(1)}, s32[]{:T(128)}, /*index=5*/bf16[8,16,128,256]{3...) while((s32[]{:T(128)}, f32[8,2048]{1,0:T(8,128)S(1)}, ...), condition=%wide.region_12.13_spmd, body=%wide.region_5.12_spmd.sunk | while | flops 277246400 | bytes 24204612 | solution.py:137
  105.4 2.0 stack.1289
  111.4 1.8 fusion.79
  119.7 2.0 stack.1289
  123.9 1.8 fusion.80
  125.7 1.8 fusion.79
  134.0 2.0 stack.1289
  138.2 1.8 fusion.80
  140.0 1.8 fusion.79
  148.3 2.0 stack.1289
  152.5 1.8 fusion.80
  154.3 1.8 fusion.79
  162.6 2.0 stack.1289
  166.8 1.8 fusion.80
  177.0 2.0 stack.1289
  181.2 1.8 fusion.80
  191.3 2.0 stack.1289
  195.5 1.8 fusion.80
  205.6 2.0 stack.1289
  209.8 1.8 fusion.80
  214.3 7.3 %collective-permute-start.3 = (f32[16384]{0:T(1024)S(1)}, f32[16384]{0:T(1024)S(1)}, u32[]{:S(2)}, u32[]{:S(2)}) collective-permute-start(f32[16384]{0:T(1024)S(1)} %slice.820), channel_id=1, source_target_pairs={{0,8},{2,10},{4,12},{6,14},{1,9},{3,11},{5,13},{7,15},{16,24},{18,... | collective-permute-start | bytes 196616 | tf_op jit(solution)/shard_map/ppermute | solution.py:20
  221.6 2.4 collective-permute-start.4
  226.2 22.0 %all-reduce.9.cloned.1.call-done = (f32[16384]{0:T(1024)}, f32[16384]{0:T(1024)}) async-done(((f32[16384]{0:T(1024)}, f32[16384]{0:T(1024)}), (f32[16384]{0:T(1024)}, f32[16384]{0:T(1024)})) %all-reduce.9.cloned.1.call-update) | async-done | bytes 131088 | tf_op jit(solution)/shard_map/pmax | solution.py:148
  (2427 shorter events, 132.5 us)
Async XLA Ops:
  7.2 241.0 %all-reduce.9.cloned.1.call-start = ((), (), s32[]{:S(2)}) async-start(), calls=%async_computation | async-start | bytes 262144 | tf_op jit(solution)/shard_map/pmax | solution.py:148
  7.9 7.2 %collective-permute-start = (f32[256]{0:T(256)S(1)}, f32[256]{0:T(256)S(1)}, u32[]{:S(2)}, u32[]{:S(2)}) collective-permute-start(f32[256]{0:T(256)S(1)} %slice.807), channel_id=1, source_target_pairs={{2,0},{4,2},{6,4},{8,6},{10,8},{12,10},{14,12},{3,1},{5,3},{7,5},{... | collective-permute-start | bytes 3080 | tf_op jit(solution)/shard_map/ppermute | solution.py:20
  9.9 89.2 %collective-permute-start.2 = (f32[4096]{0:T(1024)S(1)}, f32[4096]{0:T(1024)S(1)}, u32[]{:S(2)}, u32[]{:S(2)}) collective-permute-start(f32[4096]{0:T(1024)S(1)} %slice.808), channel_id=1, source_target_pairs={{10,0},{12,2},{14,4},{11,1},{13,3},{15,5},{26,16},{28,18},{30,20},... | collective-permute-start | bytes 49160 | tf_op jit(solution)/shard_map/ppermute | solution.py:20
  16.8 82.3 %collective-permute-start.1 = (f32[16640]{0:T(1024)S(1)}, f32[16640]{0:T(1024)S(1)}, u32[]{:S(2)}, u32[]{:S(2)}) collective-permute-start(f32[16640]{0:T(1024)S(1)} %pad_maximum_fusion.2), channel_id=1, source_target_pairs={{8,0},{10,2},{12,4},{14,6},{9,1},{11,3},{13,5},{15,7},{24,16},{26,... | collective-permute-start | bytes 199688 | tf_op jit(solution)/shard_map/ppermute | solution.py:20
  214.3 11.2 %collective-permute-start.3 = (f32[16384]{0:T(1024)S(1)}, f32[16384]{0:T(1024)S(1)}, u32[]{:S(2)}, u32[]{:S(2)}) collective-permute-start(f32[16384]{0:T(1024)S(1)} %slice.820), channel_id=1, source_target_pairs={{0,8},{2,10},{4,12},{6,14},{1,9},{3,11},{5,13},{7,15},{16,24},{18,... | collective-permute-start | bytes 196616 | tf_op jit(solution)/shard_map/ppermute | solution.py:20
  221.6 3.9 %collective-permute-start.4 = (f32[4096]{0:T(1024)S(1)}, f32[4096]{0:T(1024)S(1)}, u32[]{:S(2)}, u32[]{:S(2)}) collective-permute-start(f32[4096]{0:T(1024)S(1)} %slice.821), channel_id=1, source_target_pairs={{0,10},{2,12},{4,14},{1,11},{3,13},{5,15},{16,26},{18,28},{20,30},... | collective-permute-start | bytes 49160 | tf_op jit(solution)/shard_map/ppermute | solution.py:20
Sparse Core Ops, SparseCore 0:
  226.3 21.8 all-reduce.8
where the time goes:
time: 259 us; the launch traced here: 258 us
  local copies, waits for them, and re-layouts  111 us (43%)
  other arithmetic  39.6 us (15%)
  matrix products  28 us (11%)
  loops' own time  26.3 us (10%)
  waiting for transfers between devices  22.8 us (9%)
  between operations  16.8 us (6%)
  starting transfers between devices  13.6 us (5%)
    another operation x2064, local copies, waits for them, and re-layouts, hankel(): jnp.stack([lax.slice_in_dim(samples, offset, offset + length) for offset...  60.5 us
    slice x144, local copies, waits for them, and re-layouts, hankel(): lax.slice_in_dim(samples, offset, offset + length)  28.4 us
    pmax x1, waiting for transfers between devices, body(): return lax.pmax((row_best.reshape(block_len), col_best), 'band')  22 us
    another operation x1, loops' own time, body(): lax.map(pair_group, (jnp.arange(group_count, dtype=jnp.int32), row_z))  16.2 us
    dot_general x8, matrix products, score_group(): jnp.einsum('tim,tjm->tij', row_z, col_z[1:, :OFF_DEV], preferred_element_...  14 us
    dot_general x8, matrix products, score_group(): jnp.einsum('tim,tjm->tij', row_z, col_z[:-1], preferred_element_type=jnp....  14 us
    ppermute x5, starting transfers between devices, from_behind(): return lax.ppermute(block, axis, route)  13.6 us
    dynamic_update_slice x8, other arithmetic, body(): lax.map(own_group, jnp.arange(group_count, dtype=jnp.int32))  12.2 us
  transfers between devices with their start and end apart: 6, of which 2 were waited for; matrix products, arithmetic and copies ran while one was open for 29% of the time, Pallas kernels for 0%

commit v1 on v0

--- a/solution.py
+++ b/solution.py
@@ -1,6 +1,10 @@
+import functools
+
 import jax
 import jax.numpy as jnp
 from jax import lax
+from jax.experimental import pallas as pl
+from jax.experimental.pallas import tpu as pltpu
 from jax.sharding import PartitionSpec as P
 
 M = 256
@@ -148,10 +152,457 @@
     return lax.pmax((row_best.reshape(block_len), col_best), "band")
 
 
+SLOTS = 4
+LANES = 128
+
+
+def pair_kernel(
+    blocks,
+    starts_ref,
+    x_ref,
+    tail_ref,
+    row_out,
+    col_out,
+    ext,
+    rows_x,
+    shifted,
+    stats,
+    row_z,
+    col_z,
+    col_buf,
+    row_res,
+    col_res,
+    slots,
+    carry_in,
+    in_send,
+    in_recv,
+    out_send,
+    row_recv,
+    slot_recv,
+    carry_recv,
+):
+    half = BAND_BLOCKS
+    block_rows = x_ref.shape[0]
+    quarter = block_rows // SLOTS
+    piece = 2 * quarter + 8
+    band_count = starts_ref.shape[0]
+    p = lax.axis_index("tm")
+    b = lax.axis_index("band")
+    low = p < half
+    high = p >= half
+    partner = lax.rem(p + half, blocks)
+    part = b + 2 * (p // half)
+    first = 2 * quarter + quarter * b
+
+    def remote(src, dst, send, recv, tm, band):
+        return pltpu.make_async_remote_copy(
+            src_ref=src,
+            dst_ref=dst,
+            send_sem=send,
+            recv_sem=recv,
+            device_id={"tm": tm, "band": band},
+            device_id_type=pl.DeviceIdType.MESH,
+        )
+
+    head_sender = jnp.logical_and(p >= b, p < half + b)
+    next_sender = p > half
+    next_taker = jnp.logical_and(high, p < blocks - 1)
+    carry_sender = jnp.logical_and(next_taker, b == 1)
+    carry_taker = next_sender
+
+    barrier = pltpu.get_barrier_semaphore()
+
+    def greet(tm, band):
+        pl.semaphore_signal(
+            barrier, 1, device_id={"tm": tm, "band": band}, device_id_type=pl.DeviceIdType.MESH
+        )
+
+    greet(p, 1 - b)
+    greet(partner, 0)
+    greet(partner, 1)
+
+    @pl.when(jnp.logical_and(high, b == 1))
+    def _():
+        greet(p - half + 1, 1)
+
+    @pl.when(next_taker)
+    def _():
+        greet(p + 1, b)
+
+    @pl.when(carry_taker)
+    def _():
+        greet(p - 1, 1)
+
+    col_buf[...] = jnp.full(col_buf.shape, -1.0, jnp.float32)
+
+    @pl.when(low)
+    def _():
+        rows_x[...] = x_ref[pl.ds(pl.multiple_of(quarter * b, 8), quarter + 8), :]
+        col_out[...] = jnp.full(col_out.shape, -1.0, jnp.float32)
+
+    @pl.when(high)
+    def _():
+        ext[pl.ds(2 * quarter, 2 * quarter), :] = x_ref[pl.ds(2 * quarter, 2 * quarter), :]
+        row_out[...] = jnp.full(row_out.shape, -1.0, jnp.float32)
+
+    @pl.when(p == blocks - 1)
+    def _():
+        ext[pl.ds(block_rows, quarter + 8), :] = jnp.zeros((quarter + 8, LANES), jnp.float32)
+        ext[pl.ds(block_rows, M // LANES), :] = tail_ref[...]
+
+    head_here = jnp.where(jnp.logical_and(b == 1, jnp.logical_and(p >= 1, p <= half)), 1, 0)
+    next_here = jnp.where(next_sender, 1, 0)
+    carry_here = jnp.where(carry_sender, 2, 0)
+    pl.semaphore_wait(barrier, 3 + head_here + next_here + carry_here)
+
+    cols_copy = remote(
+        x_ref.at[pl.ds(pl.multiple_of(quarter * b, 8), piece), :],
+        ext.at[pl.ds(pl.multiple_of(first, 8), piece), :],
+        in_send.at[0],
+        in_recv.at[0],
+        partner,
+        b,
+    )
+    rows_copy = remote(
+        x_ref.at[pl.ds(pl.multiple_of(first, 8), quarter), :],
+        rows_x.at[pl.ds(0, quarter), :],
+        in_send.at[1],
+        in_recv.at[1],
+        partner,
+        b,
+    )
+    head_copy = remote(
+        x_ref.at[pl.ds(pl.multiple_of(3 * quarter * (1 - b), 8), 8), :],
+        rows_x.at[pl.ds(quarter, 8), :],
+        in_send.at[2],
+        in_recv.at[2],
+        lax.rem(p + half - b, blocks),
+        b,
+    )
+    next_copy = remote(
+        x_ref.at[pl.ds(0, quarter + 8), :],
+        ext.at[pl.ds(block_rows, quarter + 8), :],
+        in_send.at[3],
+        in_recv.at[3],
+        lax.rem(p + blocks - 1, blocks),
+        b,
+    )
+    pl.when(high)(cols_copy.start)
+    pl.when(low)(rows_copy.start)
+    pl.when(head_sender)(head_copy.start)
+    pl.when(next_sender)(next_copy.start)
+
+    pl.when(low)(cols_copy.wait_recv)
+
+    @pl.when(high)
+    def _():
+        rows_copy.wait_recv()
+        head_copy.wait_recv()
+
+    pl.when(next_taker)(next_copy.wait_recv)
+
+    span = quarter + 8
+    lane = lax.broadcasted_iota(jnp.int32, (span, LANES), 1)
+
+    def moments_of(samples):
+        mean, spread = samples, None
+        width = 1
+
+        def ahead(values):
+            below = pltpu.roll(values, span - 1, 0)
+            if width == LANES:
+                return below
+            turned = pltpu.roll(values, LANES - width, 1)
+            return jnp.where(lane < LANES - width, turned, pltpu.roll(turned, span - 1, 0))
+
+        while width < M:
+            other = ahead(mean)
+            gap = mean - other
+            term = gap * gap * (0.5 * width)
+            spread = term if spread is None else spread + ahead(spread) + term
+            mean = 0.5 * (mean + other)
+            width *= 2
+        return mean, lax.rsqrt(spread + M * EPS)
+
+    square = (LANES, LANES)
+    upper = lax.broadcasted_iota(jnp.int32, square, 1) <= lax.broadcasted_iota(jnp.int32, square, 0)
+    keep = lax.broadcasted_iota(jnp.int32, square, 1) >= lax.broadcasted_iota(jnp.int32, square, 0)
+
+    def turned_row(source, index):
+        line = source[pl.ds(index, 1), :]
+        return pltpu.roll(jnp.broadcast_to(line, square), 1, 1, stride=1, stride_axis=0)
+
+    def build(source, center, factor, count, unroll, store):
+        turn0 = turned_row(source, 0)
+        turn1 = turned_row(source, 1)
+
+        def step(index, state):
+            turn, near = state
+            following = turned_row(source, index + 2)
+            far = jnp.where(upper, turn, following)
+            c = center[pl.ds(index, 1), :]
+            f = factor[pl.ds(index, 1), :]
+            z = jnp.concatenate([(near - c) * f, (far - c) * f], axis=0)
+            store(index, z)
+            return following, far
+
+        lax.fori_loop(0, count, step, (turn1, jnp.where(upper, turn0, turn1)), unroll=unroll)
+
+    mean, factor = moments_of(rows_x[...])
+    stats[0] = mean
+    stats[1] = factor
+
+    def store_row(index, z):
+        row_z[index] = z.astype(jnp.bfloat16).T
+
+    build(rows_x, stats.at[0], stats.at[1], quarter, 2, store_row)
+
+    starts = [starts_ref[c] for c in range(band_count)]
+    whole = [lax.shift_right_logical(s, 7) for s in starts]
+    rest = [lax.bitwise_and(s, LANES - 1) for s in starts]
+    for c in range(band_count):
+        back = lax.rem(LANES - rest[c], LANES)
+        here = pltpu.roll(ext[pl.ds(first + whole[c], span), :], back, 1)
+        below = pltpu.roll(ext[pl.ds(first + whole[c] + 1, span), :], back, 1)
+        samples = jnp.where(lane < LANES - rest[c], here, below)
+        shifted[c] = samples
+        mean, factor = moments_of(samples)
+        stats[2 + 2 * c] = mean
+        stats[3 + 2 * c] = factor
+
+        def store_col(index, z, c=c):
+            col_z[c, index] = z.astype(jnp.bfloat16)
+
+        build(shifted.at[c], stats.at[2 + 2 * c], stats.at[3 + 2 * c], quarter + 1, 3, store_col)
+
+    last_block = lax.rem(p, half) + half
+    room_all = (blocks - last_block) * block_rows * LANES - part * quarter * LANES
+    lane_row = lax.broadcasted_iota(jnp.int32, (1, LANES), 1)
+
+    def score(index, pending):
+        best = None
+        left = []
+        for c in range(band_count):
+            both = jnp.concatenate([col_z[c, index], col_z[c, index + 1]], axis=1)
+            found = jnp.dot(row_z[index], both, preferred_element_type=jnp.float32)
+            room = room_all - starts[c] - index * LANES
+            near = found[:, :LANES] + jnp.where(lane_row < room, 0.0, -4.0)
+            far = found[:, LANES:] + jnp.where(lane_row + LANES < room, 0.0, -4.0)
+            near_cols = jnp.max(jnp.where(keep, near, -4.0), axis=0, keepdims=True)
+            far_cols = jnp.max(jnp.where(keep, -4.0, far), axis=0, keepdims=True)
+            col_buf[c, pl.ds(quarter + index, 1), :] = jnp.maximum(
+                jnp.maximum(pending[c], near_cols), -1.0
+            )
+            left.append(jnp.maximum(far_cols, -1.0))
+            joined = jnp.where(keep, near, far)
+            best = joined if best is None else jnp.maximum(best, joined)
+        row_res[pl.ds(index, 1), :] = jnp.maximum(jnp.max(best.T, axis=0, keepdims=True), -1.0)
+        return tuple(left)
+
+    floor = jnp.full((1, LANES), -1.0, jnp.float32)
+    pending = lax.fori_loop(0, quarter, score, (floor,) * band_count, unroll=2)
+    lane_wide = lax.broadcasted_iota(jnp.int32, (2 * quarter, LANES), 1)
+    reached = None
+    for c in range(band_count):
+        col_buf[c, pl.ds(2 * quarter, 1), :] = pending[c]
+        here = pltpu.roll(col_buf[c, pl.ds(quarter - whole[c], 2 * quarter), :], rest[c], 1)
+        above = pltpu.roll(col_buf[c, pl.ds(quarter - whole[c] - 1, 2 * quarter), :], rest[c], 1)
+        placed = jnp.where(lane_wide >= rest[c], here, above)
+        reached = placed if reached is None else jnp.maximum(reached, placed)
+    col_res[...] = reached
+
+    place = pl.ds(pl.multiple_of(part * quarter, 8), quarter)
+    row_to = [
+        remote(row_res, row_out.at[place, :], out_send.at[k], row_recv.at[part], tm, band)
+        for k, (tm, band) in enumerate([(p, 1 - b), (partner, 0), (partner, 1)])
+    ]
+    slot_to = [
+        remote(col_res, slots.at[part], out_send.at[3 + k], slot_recv.at[part], tm, band)
+        for k, (tm, band) in enumerate([(p, 1 - b), (partner, 0), (partner, 1)])
+    ]
+    lower = pl.ds(0, quarter)
+    lower_to = remote(
+        col_res.at[lower, :],
+        slots.at[part, lower, :],
+        out_send.at[3],
+        slot_recv.at[part],
+        p,
+        1 - b,
+    )
+    carry_to = [
+        remote(
+            col_res.at[pl.ds(quarter, quarter), :],
+            carry_in,
+            out_send.at[6 + k],
+            carry_recv.at[0],
+            lax.rem(p + 1, blocks),
+            k,
+        )
+        for k in range(2)
+    ]
+
+    @pl.when(low)
+    def _():
+        slot_to[1].start()
+        slot_to[2].start()
+        row_to[0].start()
+        row_out[place, :] = row_res[...]
+
+    @pl.when(high)
+    def _():
+        row_to[1].start()
+        row_to[2].start()
+
+    @pl.when(jnp.logical_and(high, b == 0))
+    def _():
+        slot_to[0].start()
+        slots[2] = col_res[...]
+
+    @pl.when(carry_sender)
+    def _():
+        carry_to[0].start()
+        carry_to[1].start()
+
+    @pl.when(jnp.logical_and(high, b == 1))
+    def _():
+        lower_to.start()
+        slots[3, lower, :] = col_res[lower, :]
+
+    def row_from(index):
+        return remote(
+            row_res,
+            row_out.at[pl.ds(index * quarter, quarter), :],
+            out_send.at[0],
+            row_recv.at[index],
+            p,
+            1 - b,
+        )
+
+    def slot_from(index):
+        return remote(
+            col_res, slots.at[index], out_send.at[0], slot_recv.at[index], p, 1 - b
+        )
+
+    @pl.when(low)
+    def _():
+        pl.when(b == 1)(row_from(0).wait_recv)
+        pl.when(b == 0)(row_from(1).wait_recv)
+        row_from(2).wait_recv()
+        row_from(3).wait_recv()
+
+    @pl.when(high)
+    def _():
+        slot_from(0).wait_recv()
+        slot_from(1).wait_recv()
+
+    @pl.when(jnp.logical_and(high, b == 1))
+    def _():
+        slot_from(2).wait_recv()
+
+    @pl.when(jnp.logical_and(high, b == 0))
+    def _():
+        remote(
+            col_res.at[lower, :],
+            slots.at[3, lower, :],
+            out_send.at[0],
+            slot_recv.at[3],
+            p,
+            1 - b,
+        ).wait_recv()
+
+    pl.when(carry_taker)(carry_to[0].wait_recv)
+
+    @pl.when(p == half)
+    def _():
+        carry_in[...] = jnp.full(carry_in.shape, -1.0, jnp.float32)
+
+    @pl.when(high)
+    def _():
+        col_out[pl.ds(0, quarter), :] = jnp.maximum(slots[0, lower, :], carry_in[...])
+        for k in range(1, SLOTS):
+            col_out[pl.ds(k * quarter, quarter), :] = jnp.maximum(
+                slots[k, lower, :], slots[k - 1, pl.ds(quarter, quarter), :]
+            )
+
+    @pl.when(high)
+    def _():
+        cols_copy.wait_send()
+        row_to[1].wait_send()
+        row_to[2].wait_send()
+
+    @pl.when(low)
+    def _():
+        rows_copy.wait_send()
+        slot_to[1].wait_send()
+        slot_to[2].wait_send()
+        row_to[0].wait_send()
+
+    pl.when(head_sender)(head_copy.wait_send)
+    pl.when(next_sender)(next_copy.wait_send)
+    pl.when(jnp.logical_and(high, b == 0))(slot_to[0].wait_send)
+    pl.when(jnp.logical_and(high, b == 1))(lower_to.wait_send)
+
+    @pl.when(carry_sender)
+    def _():
+        carry_to[0].wait_send()
+        carry_to[1].wait_send()
+
+
+def spread_body(series, tail, band_starts):
+    block_rows = series.shape[0] // LANES
+    quarter = block_rows // SLOTS
+    band_count = band_starts.shape[0]
+    blocks = lax.axis_size("tm")
+    span = quarter + 8
+    vmem = pl.BlockSpec(memory_space=pltpu.VMEM)
+    whole = jax.ShapeDtypeStruct((block_rows, LANES), jnp.float32)
+
+    def buffer(*shape, kind=jnp.float32):
+        return pltpu.VMEM(shape, kind)
+
+    best_rows, best_cols = pl.pallas_call(
+        functools.partial(pair_kernel, blocks),
+        out_shape=(whole, whole),
+        in_specs=[pl.BlockSpec(memory_space=pltpu.SMEM), vmem, vmem],
+        out_specs=(vmem, vmem),
+        scratch_shapes=[
+            buffer(block_rows + span, LANES),
+            buffer(span, LANES),
+            buffer(band_count, span, LANES),
+            buffer(2 + 2 * band_count, span, LANES),
+            buffer(quarter, LANES, M, kind=jnp.bfloat16),
+            buffer(band_count, quarter + 1, M, LANES, kind=jnp.bfloat16),
+            buffer(band_count, 3 * quarter + 8, LANES),
+            buffer(quarter, LANES),
+            buffer(2 * quarter, LANES),
+            buffer(SLOTS, 2 * quarter, LANES),
+            buffer(quarter, LANES),
+            pltpu.SemaphoreType.DMA((4,)),
+            pltpu.SemaphoreType.DMA((4,)),
+            pltpu.SemaphoreType.DMA((8,)),
+            pltpu.SemaphoreType.DMA((SLOTS,)),
+            pltpu.SemaphoreType.DMA((SLOTS,)),
+            pltpu.SemaphoreType.DMA((1,)),
+        ],
+        compiler_params=pltpu.CompilerParams(
+            collective_id=0, has_side_effects=True, vmem_limit_bytes=40 * 1024 * 1024
+        ),
+        name="banded_pairs",
+    )(band_starts, series.reshape(block_rows, LANES), tail.reshape(-1, LANES))
+    return best_rows.reshape(-1), best_cols.reshape(-1)
+
+
 def solution(mesh):
     placed = (P(("groups", "tm")), P("groups"), P("groups"))
+
+    def chosen(series, tail, band_starts):
+        halves = lax.axis_size("tm") == 2 * BAND_BLOCKS
+        if halves and series.shape[0] == SLOTS * BAND_SPAN and lax.axis_size("band") == 2:
+            return spread_body(series, tail, band_starts)
+        return body(series, tail, band_starts)
+
     return jax.shard_map(
-        body,
+        chosen,
         mesh=mesh,
         in_specs=placed,
         out_specs=(P(("groups", "tm")), P(("groups", "tm"))),

time: 259 us -> 27.4 us (0.11)
  local copies, waits for them, and re-layouts: 111 us -> 2.77 us
  other arithmetic: 39.6 us -> 0 us
  matrix products: 28 us -> 0 us
  loops' own time: 26.3 us -> 0 us
  Pallas kernels: 0 us -> 23.7 us
  waiting for transfers between devices: 22.8 us -> 0 us
  between operations: 16.8 us -> 0.66 us
  starting transfers between devices: 13.6 us -> 0 us
    another operation x2064 -> x0, local copies, waits for them, and re-layouts: 60.5 us -> none  [hankel(): jnp.stack([lax.slice_in_dim(samples, offset, offset + length) for offset...]
    slice x165 -> x0, local copies, waits for them, and re-layouts: 33.8 us -> none  [the longest x144 28.4 us: hankel(): lax.slice_in_dim(samples, offset, offset + length)]
    dot_general x16 -> x0, matrix products: 28 us -> none  [the longest x8 14 us: score_group(): jnp.einsum('tim,tjm->tij', row_z, col_z[1:, :OFF_DEV], preferred_element_...]
    another operation x2 -> x0, loops' own time: 26.3 us -> none  [the longest x1 16.2 us: body(): lax.map(pair_group, (jnp.arange(group_count, dtype=jnp.int32), row_z))]
    pallas_call x0 -> x1, Pallas kernels: none -> 23.7 us  [spread_body(): pl.pallas_call(functools.partial(pair_kernel, blocks), out_shape=(whole,...]
    pmax x1 -> x0, waiting for transfers between devices: 22 us -> none  [body(): return lax.pmax((row_best.reshape(block_len), col_best), 'band')]
    reduce_sum x33 -> x0, other arithmetic: 17.7 us -> none  [the longest x16 10.6 us: moments(): factor = lax.rsqrt(jnp.sum(spread * spread, axis=-1) + M * EPS)]
    ppermute x5 -> x0, starting transfers between devices: 13.6 us -> none  [from_behind(): return lax.ppermute(block, axis, route)]
  transfers between devices with their start and end apart: 6 -> 0, of which waited for: 2 -> 0; matrix products, arithmetic and copies ran while one was open for 29% -> 0% of each run, Pallas kernels for 0% -> 0%
where the time goes in v1:
time: 27.4 us; the launch traced here: 27.2 us
  Pallas kernels  23.7 us (86%)
  local copies, waits for them, and re-layouts  2.77 us (10%)
  between operations  0.66 us (2%)
    pallas_call x1, Pallas kernels, spread_body(): pl.pallas_call(functools.partial(pair_kernel, blocks), out_shape=(whole,...  23.7 us
    unnamed x8, local copies, waits for them, and re-layouts  2.77 us

profile of v1, /device:TPU:0, one launch (start us, length us, event | category | flops | bytes accessed | tf_op | source)
XLA Modules:
  0.0 27.2 jit_solution(3189873216809151095)
XLA Ops:
  0.6 0.0 copy-start.1
  0.6 0.0 copy-start.2
  0.6 0.7 %copy-done.1 = f32[256]{0:T(256)S(1)} copy-done((f32[256]{0:T(256)S(1)}, f32[256]{0:T(256)}, u32[]{:S(2)}) %copy-start.1) | copy-done | bytes 1048
  1.3 0.0 copy-done.2
  1.3 0.0 copy-start
  1.3 0.8 %copy-done = f32[16384]{0:T(1024)S(1)} copy-done((f32[16384]{0:T(1024)S(1)}, f32[16384]{0:T(1024)}, u32[]{:S(2)}) %copy-start) | copy-done | bytes 65560
  2.2 23.7 %banded_pairs.1 = (f32[128,128]{1,0:T(8,128)S(1)}, f32[128,128]{1,0:T(8,128)S(1)}) custom-call(s32[2]{0:T(128)S(1)} %copy-done.2, f32[128,128]{1,0:T(8,128)S(1)} %bitcast.4, f32[2,128]{1,0:T(2,128)S(1)} %bitcast.7), custom_call_target="tpu_custom_call" | custom-call | tf_op jit(solution)/shard_map/banded_pairs/pallas_call | solution.py:563
  25.9 0.6 %copy.7 = f32[16384]{0:T(1024)} copy(f32[16384]{0:T(1024)S(1)} %bitcast.6) | data formatting | bytes 131072
  26.5 0.6 %copy.8 = f32[16384]{0:T(1024)} copy(f32[16384]{0:T(1024)S(1)} %bitcast.5) | data formatting | bytes 131072
Async XLA Ops:
  0.6 0.7 %copy-start.1 = (f32[256]{0:T(256)S(1)}, f32[256]{0:T(256)}, u32[]{:S(2)}) copy-start(f32[256]{0:T(256)} %param.4) | copy-start | bytes 3076
  0.6 0.7 %copy-start.2 = (s32[2]{0:T(128)S(1)}, s32[2]{0:T(128)}, u32[]{:S(2)}) copy-start(s32[2]{0:T(128)} %starts_ref.1) | copy-start | bytes 28
  1.3 0.8 %copy-start = (f32[16384]{0:T(1024)S(1)}, f32[16384]{0:T(1024)}, u32[]{:S(2)}) copy-start(f32[16384]{0:T(1024)} %param.3) | copy-start | bytes 196612

commit v2 on v1

--- a/solution.py
+++ b/solution.py
@@ -158,15 +158,18 @@
 
 def pair_kernel(
     blocks,
-    starts_ref,
+    starts_in,
     x_ref,
     tail_ref,
     row_out,
     col_out,
+    starts_ref,
     ext,
     rows_x,
+    rows_back,
     shifted,
     stats,
+    across,
     row_z,
     col_z,
     col_buf,
@@ -174,6 +177,7 @@
     col_res,
     slots,
     carry_in,
+    local,
     in_send,
     in_recv,
     out_send,
@@ -233,22 +237,36 @@
     def _():
         greet(p - 1, 1)
 
+    starts_copy = pltpu.make_async_copy(starts_in, starts_ref, local.at[0])
+    own_rows = pltpu.make_async_copy(
+        x_ref.at[pl.ds(pl.multiple_of(quarter * b, 8), quarter + 8), :], rows_x, local.at[1]
+    )
+    own_cols = pltpu.make_async_copy(
+        x_ref.at[pl.ds(2 * quarter, 2 * quarter), :],
+        ext.at[pl.ds(2 * quarter, 2 * quarter), :],
+        local.at[1],
+    )
+    own_tail = pltpu.make_async_copy(
+        tail_ref, ext.at[pl.ds(block_rows, M // LANES), :], local.at[2]
+    )
+    starts_copy.start()
+    pl.when(low)(own_rows.start)
+    pl.when(high)(own_cols.start)
+
+    @pl.when(p == blocks - 1)
+    def _():
+        ext[pl.ds(block_rows, quarter + 8), :] = jnp.zeros((quarter + 8, LANES), jnp.float32)
+        own_tail.start()
+
     col_buf[...] = jnp.full(col_buf.shape, -1.0, jnp.float32)
 
     @pl.when(low)
     def _():
-        rows_x[...] = x_ref[pl.ds(pl.multiple_of(quarter * b, 8), quarter + 8), :]
         col_out[...] = jnp.full(col_out.shape, -1.0, jnp.float32)
 
     @pl.when(high)
     def _():
-        ext[pl.ds(2 * quarter, 2 * quarter), :] = x_ref[pl.ds(2 * quarter, 2 * quarter), :]
         row_out[...] = jnp.full(row_out.shape, -1.0, jnp.float32)
-
-    @pl.when(p == blocks - 1)
-    def _():
-        ext[pl.ds(block_rows, quarter + 8), :] = jnp.zeros((quarter + 8, LANES), jnp.float32)
-        ext[pl.ds(block_rows, M // LANES), :] = tail_ref[...]
 
     head_here = jnp.where(jnp.logical_and(b == 1, jnp.logical_and(p >= 1, p <= half)), 1, 0)
     next_here = jnp.where(next_sender, 1, 0)
@@ -292,15 +310,7 @@
     pl.when(head_sender)(head_copy.start)
     pl.when(next_sender)(next_copy.start)
 
-    pl.when(low)(cols_copy.wait_recv)
-
-    @pl.when(high)
-    def _():
-        rows_copy.wait_recv()
-        head_copy.wait_recv()
-
-    pl.when(next_taker)(next_copy.wait_recv)
-
+    starts_copy.wait()
     span = quarter + 8
     lane = lax.broadcasted_iota(jnp.int32, (span, LANES), 1)
 
@@ -332,54 +342,123 @@
         line = source[pl.ds(index, 1), :]
         return pltpu.roll(jnp.broadcast_to(line, square), 1, 1, stride=1, stride_axis=0)
 
-    def build(source, center, factor, count, unroll, store):
-        turn0 = turned_row(source, 0)
-        turn1 = turned_row(source, 1)
+    lane_quarter = lax.broadcasted_iota(jnp.int32, (LANES, quarter), 1)
+
+    def build_rows():
+        samples = rows_x[...]
+        mean, factor = moments_of(samples)
+        across[0] = mean[:quarter].T
+        across[1] = factor[:quarter].T
+        flip = jnp.where(
+            lax.broadcasted_iota(jnp.int32, square, 0) + lax.broadcasted_iota(jnp.int32, square, 1)
+            == LANES - 1,
+            1.0,
+            0.0,
+        ).astype(jnp.bfloat16)
+        left = samples
+        back = None
+        for _ in range(3):
+            some = left.astype(jnp.bfloat16)
+            left = left - some.astype(jnp.float32)
+            moved = jnp.dot(some, flip, preferred_element_type=jnp.float32)
+            back = moved if back is None else back + moved
+        rows_back[...] = back
+
+        def turned(index):
+            line = rows_back[pl.ds(index, 1), :]
+            return pltpu.roll(jnp.broadcast_to(line, square), 0, 1, stride=1, stride_axis=0)
+
+        def column(which, index):
+            return jnp.sum(
+                jnp.where(lane_quarter == index, across[which], 0.0), axis=1, keepdims=True
+            )
+
+        turn0 = turned(0)
+        turn1 = turned(1)
 
         def step(index, state):
             turn, near = state
-            following = turned_row(source, index + 2)
-            far = jnp.where(upper, turn, following)
-            c = center[pl.ds(index, 1), :]
-            f = factor[pl.ds(index, 1), :]
-            z = jnp.concatenate([(near - c) * f, (far - c) * f], axis=0)
-            store(index, z)
+            following = turned(index + 2)
+            far = jnp.where(keep, turn, following)
+            c = column(0, index)
+            f = column(1, index)
+            row_z[index, :, :LANES] = ((near - c) * f).astype(jnp.bfloat16)
+            row_z[index, :, LANES:] = ((far - c) * f).astype(jnp.bfloat16)
             return following, far
 
-        lax.fori_loop(0, count, step, (turn1, jnp.where(upper, turn0, turn1)), unroll=unroll)
-
-    mean, factor = moments_of(rows_x[...])
-    stats[0] = mean
-    stats[1] = factor
-
-    def store_row(index, z):
-        row_z[index] = z.astype(jnp.bfloat16).T
-
-    build(rows_x, stats.at[0], stats.at[1], quarter, 2, store_row)
+        lax.fori_loop(0, quarter, step, (turn1, jnp.where(keep, turn0, turn1)), unroll=4)
 
     starts = [starts_ref[c] for c in range(band_count)]
     whole = [lax.shift_right_logical(s, 7) for s in starts]
     rest = [lax.bitwise_and(s, LANES - 1) for s in starts]
-    for c in range(band_count):
-        back = lax.rem(LANES - rest[c], LANES)
-        here = pltpu.roll(ext[pl.ds(first + whole[c], span), :], back, 1)
-        below = pltpu.roll(ext[pl.ds(first + whole[c] + 1, span), :], back, 1)
-        samples = jnp.where(lane < LANES - rest[c], here, below)
-        shifted[c] = samples
-        mean, factor = moments_of(samples)
-        stats[2 + 2 * c] = mean
-        stats[3 + 2 * c] = factor
-
-        def store_col(index, z, c=c):
-            col_z[c, index] = z.astype(jnp.bfloat16)
-
-        build(shifted.at[c], stats.at[2 + 2 * c], stats.at[3 + 2 * c], quarter + 1, 3, store_col)
+
+    def build_cols():
+        for c in range(band_count):
+            back = lax.rem(LANES - rest[c], LANES)
+            here = pltpu.roll(ext[pl.ds(first + whole[c], span), :], back, 1)
+            below = pltpu.roll(ext[pl.ds(first + whole[c] + 1, span), :], back, 1)
+            samples = jnp.where(lane < LANES - rest[c], here, below)
+            shifted[c] = samples
+            mean, factor = moments_of(samples)
+            stats[2 * c] = mean
+            stats[2 * c + 1] = factor
+
+        def turned(c, index):
+            line = shifted[c, pl.ds(index, 1), :]
+            return pltpu.roll(jnp.broadcast_to(line, square), 1, 1, stride=1, stride_axis=0)
+
+        for c in range(band_count):
+            turn0 = turned(c, 0)
+            turn1 = turned(c, 1)
+
+            def step(index, state, c=c):
+                turn, near = state
+                following = turned(c, index + 2)
+                far = jnp.where(upper, turn, following)
+                center = stats[2 * c, pl.ds(index, 1), :]
+                factor = stats[2 * c + 1, pl.ds(index, 1), :]
+                col_z[c, index, :LANES, :] = ((near - center) * factor).astype(jnp.bfloat16)
+                col_z[c, index, LANES:, :] = ((far - center) * factor).astype(jnp.bfloat16)
+                return following, far
+
+            lax.fori_loop(
+                0, quarter + 1, step, (turn1, jnp.where(upper, turn0, turn1)), unroll=3
+            )
+
+    def phase(turn, _):
+        rows_now = lax.rem(turn + p // half, 2) == 0
+
+        @pl.when(rows_now)
+        def _():
+            pl.when(low)(own_rows.wait)
+
+            @pl.when(high)
+            def _():
+                rows_copy.wait_recv()
+                head_copy.wait_recv()
+
+            build_rows()
+
+        @pl.when(jnp.logical_not(rows_now))
+        def _():
+            pl.when(low)(cols_copy.wait_recv)
+            pl.when(high)(own_cols.wait)
+            pl.when(next_taker)(next_copy.wait_recv)
+            pl.when(p == blocks - 1)(own_tail.wait)
+            build_cols()
+
+        return 0
+
+    lax.fori_loop(0, 2, phase, 0)
 
     last_block = lax.rem(p, half) + half
     room_all = (blocks - last_block) * block_rows * LANES - part * quarter * LANES
     lane_row = lax.broadcasted_iota(jnp.int32, (1, LANES), 1)
 
-    def score(index, pending):
+    lane_square = lax.broadcasted_iota(jnp.int32, square, 1)
+
+    def score(index, state):
+        pending, rows_found = state
         best = None
         left = []
         for c in range(band_count):
@@ -396,11 +475,16 @@
             left.append(jnp.maximum(far_cols, -1.0))
             joined = jnp.where(keep, near, far)
             best = joined if best is None else jnp.maximum(best, joined)
-        row_res[pl.ds(index, 1), :] = jnp.maximum(jnp.max(best.T, axis=0, keepdims=True), -1.0)
-        return tuple(left)
+        rows_found = jnp.where(
+            lane_square == index, jnp.max(best, axis=1, keepdims=True), rows_found
+        )
+        return tuple(left), rows_found
 
     floor = jnp.full((1, LANES), -1.0, jnp.float32)
-    pending = lax.fori_loop(0, quarter, score, (floor,) * band_count, unroll=2)
+    pending, rows_found = lax.fori_loop(
+        0, quarter, score, ((floor,) * band_count, jnp.full(square, -1.0, jnp.float32)), unroll=4
+    )
+    row_res[...] = jnp.maximum(rows_found.T[:quarter], -1.0)
     lane_wide = lax.broadcasted_iota(jnp.int32, (2 * quarter, LANES), 1)
     reached = None
     for c in range(band_count):
@@ -563,13 +647,16 @@
     best_rows, best_cols = pl.pallas_call(
         functools.partial(pair_kernel, blocks),
         out_shape=(whole, whole),
-        in_specs=[pl.BlockSpec(memory_space=pltpu.SMEM), vmem, vmem],
+        in_specs=[pl.BlockSpec(memory_space=pltpu.HBM)] * 3,
         out_specs=(vmem, vmem),
         scratch_shapes=[
+            pltpu.SMEM((band_count,), jnp.int32),
             buffer(block_rows + span, LANES),
             buffer(span, LANES),
+            buffer(span, LANES),
             buffer(band_count, span, LANES),
-            buffer(2 + 2 * band_count, span, LANES),
+            buffer(2 * band_count, span, LANES),
+            buffer(2, LANES, quarter),
             buffer(quarter, LANES, M, kind=jnp.bfloat16),
             buffer(band_count, quarter + 1, M, LANES, kind=jnp.bfloat16),
             buffer(band_count, 3 * quarter + 8, LANES),
@@ -577,6 +664,7 @@
             buffer(2 * quarter, LANES),
             buffer(SLOTS, 2 * quarter, LANES),
             buffer(quarter, LANES),
+            pltpu.SemaphoreType.DMA((3,)),
             pltpu.SemaphoreType.DMA((4,)),
             pltpu.SemaphoreType.DMA((4,)),
             pltpu.SemaphoreType.DMA((8,)),
@@ -585,7 +673,7 @@
             pltpu.SemaphoreType.DMA((1,)),
         ],
         compiler_params=pltpu.CompilerParams(
-            collective_id=0, has_side_effects=True, vmem_limit_bytes=40 * 1024 * 1024
+            collective_id=0, has_side_effects=True, vmem_limit_bytes=64 * 1024 * 1024 - 32768
         ),
         name="banded_pairs",
     )(band_starts, series.reshape(block_rows, LANES), tail.reshape(-1, LANES))

time: 27.4 us -> 24.4 us (0.89)
  Pallas kernels: 23.7 us -> 21.3 us
  local copies, waits for them, and re-layouts: 2.77 us -> 2.14 us
    pallas_call x1, Pallas kernels: 23.7 us -> 21.3 us  [spread_body(): pl.pallas_call(functools.partial(pair_kernel, blocks), out_shape=(whole,...]
    unnamed x8 -> x4, local copies, waits for them, and re-layouts: 2.77 us -> 2.14 us
where the time goes in v2:
time: 24.4 us; the launch traced here: 24.1 us
  Pallas kernels  21.3 us (87%)
  local copies, waits for them, and re-layouts  2.14 us (9%)
  between operations  0.65 us (3%)
    pallas_call x1, Pallas kernels, spread_body(): pl.pallas_call(functools.partial(pair_kernel, blocks), out_shape=(whole,...  21.3 us
    unnamed x4, local copies, waits for them, and re-layouts  2.14 us

profile of v2, /device:TPU:0, one launch (start us, length us, event | category | flops | bytes accessed | tf_op | source)
XLA Modules:
  0.0 24.1 jit_solution(4233479760942738304)
XLA Ops:
  0.6 21.3 %banded_pairs.1 = (f32[128,128]{1,0:T(8,128)}, f32[128,128]{1,0:T(8,128)}) custom-call(s32[2]{0:T(128)} %starts_in.1, f32[128,128]{1,0:T(8,128)} %bitcast.4, f32[2,128]{1,0:T(2,128)} %bitcast.7), custom_call_target="tpu_custom_call" | custom-call | tf_op jit(solution)/shard_map/banded_pairs/pallas_call | solution.py:647
  22.0 0.0 copy-start
  22.0 1.5 %copy.7 = f32[16384]{0:T(1024)} copy(f32[16384]{0:T(1024)} %bitcast.6) | data formatting | bytes 131072
  23.5 0.0 copy-done
  23.5 0.6 %copy.8 = f32[16384]{0:T(1024)} copy(f32[16384]{0:T(1024)S(1)} %bitcast.5) | data formatting | bytes 131072
Async XLA Ops:
  22.0 1.5 %copy-start = (f32[128,128]{1,0:T(8,128)S(1)}, f32[128,128]{1,0:T(8,128)}, u32[]{:S(2)}) copy-start(f32[128,128]{1,0:T(8,128)} %get-tuple-element.5) | copy-start | bytes 196612

commit v3 on v2

--- a/solution.py
+++ b/solution.py
@@ -153,6 +153,7 @@
 
 
 SLOTS = 4
+STRIP = 16
 LANES = 128
 
 
@@ -335,14 +336,15 @@
         return mean, lax.rsqrt(spread + M * EPS)
 
     square = (LANES, LANES)
-    upper = lax.broadcasted_iota(jnp.int32, square, 1) <= lax.broadcasted_iota(jnp.int32, square, 0)
     keep = lax.broadcasted_iota(jnp.int32, square, 1) >= lax.broadcasted_iota(jnp.int32, square, 0)
 
     def turned_row(source, index):
         line = source[pl.ds(index, 1), :]
         return pltpu.roll(jnp.broadcast_to(line, square), 1, 1, stride=1, stride_axis=0)
 
-    lane_quarter = lax.broadcasted_iota(jnp.int32, (LANES, quarter), 1)
+    strip_lane = lax.broadcasted_iota(jnp.int32, (STRIP, LANES), 1)
+    strip_row = lax.broadcasted_iota(jnp.int32, (STRIP, LANES), 0)
+    strip_quarter = lax.broadcasted_iota(jnp.int32, (STRIP, quarter), 1)
 
     def build_rows():
         samples = rows_x[...]
@@ -364,29 +366,45 @@
             back = moved if back is None else back + moved
         rows_back[...] = back
 
-        def turned(index):
-            line = rows_back[pl.ds(index, 1), :]
-            return pltpu.roll(jnp.broadcast_to(line, square), 0, 1, stride=1, stride_axis=0)
-
-        def column(which, index):
-            return jnp.sum(
-                jnp.where(lane_quarter == index, across[which], 0.0), axis=1, keepdims=True
+        for top in range(0, LANES, STRIP):
+            strip = pl.ds(top, STRIP)
+            inside = strip_lane >= strip_row + top
+            centers = across[0, strip, :]
+            factors = across[1, strip, :]
+
+            def turned(index, top=top):
+                line = rows_back[pl.ds(index, 1), :]
+                return pltpu.roll(
+                    jnp.broadcast_to(line, (STRIP, LANES)), top, 1, stride=1, stride_axis=0
+                )
+
+            def column(values, index):
+                chosen = jnp.where(strip_quarter == index, values, 0.0)
+                return jnp.sum(chosen, axis=1, keepdims=True)
+
+            def step(
+                index,
+                state,
+                strip=strip,
+                inside=inside,
+                centers=centers,
+                factors=factors,
+                turned=turned,
+            ):
+                turn, near = state
+                following = turned(index + 2)
+                far = jnp.where(inside, turn, following)
+                c = column(centers, index)
+                f = column(factors, index)
+                row_z[index, strip, :LANES] = ((near - c) * f).astype(jnp.bfloat16)
+                row_z[index, strip, LANES:] = ((far - c) * f).astype(jnp.bfloat16)
+                return following, far
+
+            turn0 = turned(0)
+            turn1 = turned(1)
+            lax.fori_loop(
+                0, quarter, step, (turn1, jnp.where(inside, turn0, turn1)), unroll=8
             )
-
-        turn0 = turned(0)
-        turn1 = turned(1)
-
-        def step(index, state):
-            turn, near = state
-            following = turned(index + 2)
-            far = jnp.where(keep, turn, following)
-            c = column(0, index)
-            f = column(1, index)
-            row_z[index, :, :LANES] = ((near - c) * f).astype(jnp.bfloat16)
-            row_z[index, :, LANES:] = ((far - c) * f).astype(jnp.bfloat16)
-            return following, far
-
-        lax.fori_loop(0, quarter, step, (turn1, jnp.where(keep, turn0, turn1)), unroll=4)
 
     starts = [starts_ref[c] for c in range(band_count)]
     whole = [lax.shift_right_logical(s, 7) for s in starts]
@@ -403,27 +421,38 @@
             stats[2 * c] = mean
             stats[2 * c + 1] = factor
 
-        def turned(c, index):
-            line = shifted[c, pl.ds(index, 1), :]
-            return pltpu.roll(jnp.broadcast_to(line, square), 1, 1, stride=1, stride_axis=0)
-
-        for c in range(band_count):
-            turn0 = turned(c, 0)
-            turn1 = turned(c, 1)
-
-            def step(index, state, c=c):
-                turn, near = state
-                following = turned(c, index + 2)
-                far = jnp.where(upper, turn, following)
-                center = stats[2 * c, pl.ds(index, 1), :]
-                factor = stats[2 * c + 1, pl.ds(index, 1), :]
-                col_z[c, index, :LANES, :] = ((near - center) * factor).astype(jnp.bfloat16)
-                col_z[c, index, LANES:, :] = ((far - center) * factor).astype(jnp.bfloat16)
-                return following, far
-
-            lax.fori_loop(
-                0, quarter + 1, step, (turn1, jnp.where(upper, turn0, turn1)), unroll=3
-            )
+        for top in range(0, LANES, STRIP):
+            strip = pl.ds(top, STRIP)
+            strip_far = pl.ds(LANES + top, STRIP)
+            inside = strip_lane <= strip_row + top
+
+            def turned(c, index, top=top):
+                line = shifted[c, pl.ds(index, 1), :]
+                return pltpu.roll(
+                    jnp.broadcast_to(line, (STRIP, LANES)), top + 1, 1, stride=1, stride_axis=0
+                )
+
+            def step(
+                index, state, strip=strip, strip_far=strip_far, inside=inside, turned=turned
+            ):
+                after = []
+                for c in range(band_count):
+                    turn, near = state[c]
+                    following = turned(c, index + 2)
+                    far = jnp.where(inside, turn, following)
+                    center = stats[2 * c, pl.ds(index, 1), :]
+                    factor = stats[2 * c + 1, pl.ds(index, 1), :]
+                    col_z[c, index, strip, :] = ((near - center) * factor).astype(jnp.bfloat16)
+                    col_z[c, index, strip_far, :] = ((far - center) * factor).astype(jnp.bfloat16)
+                    after.append((following, far))
+                return tuple(after)
+
+            begin = []
+            for c in range(band_count):
+                turn0 = turned(c, 0)
+                turn1 = turned(c, 1)
+                begin.append((turn1, jnp.where(inside, turn0, turn1)))
+            lax.fori_loop(0, quarter + 1, step, tuple(begin), unroll=11)
 
     def phase(turn, _):
         rows_now = lax.rem(turn + p // half, 2) == 0
@@ -640,6 +669,8 @@
     span = quarter + 8
     vmem = pl.BlockSpec(memory_space=pltpu.VMEM)
     whole = jax.ShapeDtypeStruct((block_rows, LANES), jnp.float32)
+
+    operands = (band_starts, series.reshape(block_rows, LANES), tail.reshape(-1, LANES))
 
     def buffer(*shape, kind=jnp.float32):
         return pltpu.VMEM(shape, kind)
@@ -673,10 +704,10 @@
             pltpu.SemaphoreType.DMA((1,)),
         ],
         compiler_params=pltpu.CompilerParams(
-            collective_id=0, has_side_effects=True, vmem_limit_bytes=64 * 1024 * 1024 - 32768
+            collective_id=0, has_side_effects=True, vmem_limit_bytes=40 * 1024 * 1024
         ),
         name="banded_pairs",
-    )(band_starts, series.reshape(block_rows, LANES), tail.reshape(-1, LANES))
+    )(*[pltpu.with_memory_space_constraint(a, pltpu.HBM) for a in operands])
     return best_rows.reshape(-1), best_cols.reshape(-1)
 
 

time: 24.4 us -> 28.7 us (1.18)
  Pallas kernels: 21.3 us -> 26.5 us
  local copies, waits for them, and re-layouts: 2.14 us -> 1.27 us
    pallas_call x1, Pallas kernels: 21.3 us -> 26.5 us  [spread_body(): pl.pallas_call(functools.partial(pair_kernel, blocks), out_shape=(whole,...]
    unnamed x4 -> x2, local copies, waits for them, and re-layouts: 2.14 us -> 1.27 us
where the time goes in v3:
time: 28.7 us; the launch traced here: 28.4 us
  Pallas kernels  26.5 us (92%)
  local copies, waits for them, and re-layouts  1.27 us (4%)
  between operations  0.64 us (2%)
    pallas_call x1, Pallas kernels, spread_body(): pl.pallas_call(functools.partial(pair_kernel, blocks), out_shape=(whole,...  26.5 us
    unnamed x2, local copies, waits for them, and re-layouts  1.27 us

profile of v3, /device:TPU:0, one launch (start us, length us, event | category | flops | bytes accessed | tf_op | source)
XLA Modules:
  0.0 28.4 jit_solution(15973944066271088430)
XLA Ops:
  0.6 26.5 %banded_pairs.1 = (f32[128,128]{1,0:T(8,128)S(1)}, f32[128,128]{1,0:T(8,128)S(1)}) custom-call(s32[2]{0:T(128)} %starts_in.1, f32[128,128]{1,0:T(8,128)} %bitcast.6, f32[2,128]{1,0:T(2,128)} %bitcast.7), custom_call_target="tpu_custom_call" | custom-call | tf_op jit(solution)/shard_map/banded_pairs/pallas_call | solution.py:678
  27.2 0.6 %copy.7 = f32[16384]{0:T(1024)} copy(f32[16384]{0:T(1024)S(1)} %bitcast.5) | data formatting | bytes 131072
  27.8 0.6 %copy.8 = f32[16384]{0:T(1024)} copy(f32[16384]{0:T(1024)S(1)} %bitcast.4) | data formatting | bytes 131072

commit v4 on v2

--- a/solution.py
+++ b/solution.py
@@ -386,7 +386,7 @@
             row_z[index, :, LANES:] = ((far - c) * f).astype(jnp.bfloat16)
             return following, far
 
-        lax.fori_loop(0, quarter, step, (turn1, jnp.where(keep, turn0, turn1)), unroll=4)
+        lax.fori_loop(0, quarter, step, (turn1, jnp.where(keep, turn0, turn1)), unroll=8)
 
     starts = [starts_ref[c] for c in range(band_count)]
     whole = [lax.shift_right_logical(s, 7) for s in starts]
@@ -407,11 +407,11 @@
             line = shifted[c, pl.ds(index, 1), :]
             return pltpu.roll(jnp.broadcast_to(line, square), 1, 1, stride=1, stride_axis=0)
 
-        for c in range(band_count):
+        def one_band(c, _):
             turn0 = turned(c, 0)
             turn1 = turned(c, 1)
 
-            def step(index, state, c=c):
+            def step(index, state):
                 turn, near = state
                 following = turned(c, index + 2)
                 far = jnp.where(upper, turn, following)
@@ -422,8 +422,11 @@
                 return following, far
 
             lax.fori_loop(
-                0, quarter + 1, step, (turn1, jnp.where(upper, turn0, turn1)), unroll=3
+                0, quarter + 1, step, (turn1, jnp.where(upper, turn0, turn1)), unroll=11
             )
+            return 0
+
+        lax.fori_loop(0, band_count, one_band, 0)
 
     def phase(turn, _):
         rows_now = lax.rem(turn + p // half, 2) == 0
@@ -482,7 +485,7 @@
 
     floor = jnp.full((1, LANES), -1.0, jnp.float32)
     pending, rows_found = lax.fori_loop(
-        0, quarter, score, ((floor,) * band_count, jnp.full(square, -1.0, jnp.float32)), unroll=4
+        0, quarter, score, ((floor,) * band_count, jnp.full(square, -1.0, jnp.float32)), unroll=8
     )
     row_res[...] = jnp.maximum(rows_found.T[:quarter], -1.0)
     lane_wide = lax.broadcasted_iota(jnp.int32, (2 * quarter, LANES), 1)
@@ -640,6 +643,8 @@
     span = quarter + 8
     vmem = pl.BlockSpec(memory_space=pltpu.VMEM)
     whole = jax.ShapeDtypeStruct((block_rows, LANES), jnp.float32)
+
+    operands = (band_starts, series.reshape(block_rows, LANES), tail.reshape(-1, LANES))
 
     def buffer(*shape, kind=jnp.float32):
         return pltpu.VMEM(shape, kind)
@@ -673,10 +678,10 @@
             pltpu.SemaphoreType.DMA((1,)),
         ],
         compiler_params=pltpu.CompilerParams(
-            collective_id=0, has_side_effects=True, vmem_limit_bytes=64 * 1024 * 1024 - 32768
+            collective_id=0, has_side_effects=True, vmem_limit_bytes=40 * 1024 * 1024
         ),
         name="banded_pairs",
-    )(band_starts, series.reshape(block_rows, LANES), tail.reshape(-1, LANES))
+    )(*[pltpu.with_memory_space_constraint(a, pltpu.HBM) for a in operands])
     return best_rows.reshape(-1), best_cols.reshape(-1)
 
 

time: 24.4 us -> 20.6 us (0.84)
  Pallas kernels: 21.3 us -> 18.5 us
  local copies, waits for them, and re-layouts: 2.14 us -> 1.27 us
    pallas_call x1, Pallas kernels: 21.3 us -> 18.5 us  [spread_body(): pl.pallas_call(functools.partial(pair_kernel, blocks), out_shape=(whole,...]
    unnamed x4 -> x2, local copies, waits for them, and re-layouts: 2.14 us -> 1.27 us
where the time goes in v4:
time: 20.6 us; the launch traced here: 20.4 us
  Pallas kernels  18.5 us (90%)
  local copies, waits for them, and re-layouts  1.27 us (6%)
  between operations  0.64 us (3%)
    pallas_call x1, Pallas kernels, spread_body(): pl.pallas_call(functools.partial(pair_kernel, blocks), out_shape=(whole,...  18.5 us
    unnamed x2, local copies, waits for them, and re-layouts  1.27 us

profile of v4, /device:TPU:0, one launch (start us, length us, event | category | flops | bytes accessed | tf_op | source)
XLA Modules:
  0.0 20.4 jit_solution(6279727589266665772)
XLA Ops:
  0.6 18.5 %banded_pairs.1 = (f32[128,128]{1,0:T(8,128)S(1)}, f32[128,128]{1,0:T(8,128)S(1)}) custom-call(s32[2]{0:T(128)} %starts_in.1, f32[128,128]{1,0:T(8,128)} %bitcast.6, f32[2,128]{1,0:T(2,128)} %bitcast.7), custom_call_target="tpu_custom_call" | custom-call | tf_op jit(solution)/shard_map/banded_pairs/pallas_call | solution.py:652
  19.1 0.6 %copy.7 = f32[16384]{0:T(1024)} copy(f32[16384]{0:T(1024)S(1)} %bitcast.5) | data formatting | bytes 131072
  19.7 0.6 %copy.8 = f32[16384]{0:T(1024)} copy(f32[16384]{0:T(1024)S(1)} %bitcast.4) | data formatting | bytes 131072

commit v5 on v4

--- a/solution.py
+++ b/solution.py
@@ -386,7 +386,7 @@
             row_z[index, :, LANES:] = ((far - c) * f).astype(jnp.bfloat16)
             return following, far
 
-        lax.fori_loop(0, quarter, step, (turn1, jnp.where(keep, turn0, turn1)), unroll=8)
+        lax.fori_loop(0, quarter, step, (turn1, jnp.where(keep, turn0, turn1)), unroll=16)
 
     starts = [starts_ref[c] for c in range(band_count)]
     whole = [lax.shift_right_logical(s, 7) for s in starts]
@@ -422,7 +422,7 @@
                 return following, far
 
             lax.fori_loop(
-                0, quarter + 1, step, (turn1, jnp.where(upper, turn0, turn1)), unroll=11
+                0, quarter + 1, step, (turn1, jnp.where(upper, turn0, turn1)), unroll=33
             )
             return 0
 
@@ -485,7 +485,7 @@
 
     floor = jnp.full((1, LANES), -1.0, jnp.float32)
     pending, rows_found = lax.fori_loop(
-        0, quarter, score, ((floor,) * band_count, jnp.full(square, -1.0, jnp.float32)), unroll=8
+        0, quarter, score, ((floor,) * band_count, jnp.full(square, -1.0, jnp.float32)), unroll=16
     )
     row_res[...] = jnp.maximum(rows_found.T[:quarter], -1.0)
     lane_wide = lax.broadcasted_iota(jnp.int32, (2 * quarter, LANES), 1)

time: 20.6 us -> 19.6 us (0.951)
  Pallas kernels: 18.5 us -> 17.5 us
    pallas_call x1, Pallas kernels: 18.5 us -> 17.5 us  [spread_body(): pl.pallas_call(functools.partial(pair_kernel, blocks), out_shape=(whole,...]
where the time goes in v5:
time: 19.6 us; the launch traced here: 19.4 us
  Pallas kernels  17.5 us (89%)
  local copies, waits for them, and re-layouts  1.27 us (6%)
  between operations  0.64 us (3%)
    pallas_call x1, Pallas kernels, spread_body(): pl.pallas_call(functools.partial(pair_kernel, blocks), out_shape=(whole,...  17.5 us
    unnamed x2, local copies, waits for them, and re-layouts  1.27 us

profile of v5, /device:TPU:0, one launch (start us, length us, event | category | flops | bytes accessed | tf_op | source)
XLA Modules:
  0.0 19.4 jit_solution(2459849709072209147)
XLA Ops:
  0.6 17.5 %banded_pairs.1 = (f32[128,128]{1,0:T(8,128)S(1)}, f32[128,128]{1,0:T(8,128)S(1)}) custom-call(s32[2]{0:T(128)} %starts_in.1, f32[128,128]{1,0:T(8,128)} %bitcast.6, f32[2,128]{1,0:T(2,128)} %bitcast.7), custom_call_target="tpu_custom_call" | custom-call | tf_op jit(solution)/shard_map/banded_pairs/pallas_call | solution.py:652
  18.1 0.6 %copy.7 = f32[16384]{0:T(1024)} copy(f32[16384]{0:T(1024)S(1)} %bitcast.5) | data formatting | bytes 131072
  18.7 0.6 %copy.8 = f32[16384]{0:T(1024)} copy(f32[16384]{0:T(1024)S(1)} %bitcast.4) | data formatting | bytes 131072

commit v6 on v5

--- a/solution.py
+++ b/solution.py
@@ -161,8 +161,7 @@
     starts_in,
     x_ref,
     tail_ref,
-    row_out,
-    col_out,
+    both_out,
     starts_ref,
     ext,
     rows_x,
@@ -190,6 +189,8 @@
     quarter = block_rows // SLOTS
     piece = 2 * quarter + 8
     band_count = starts_ref.shape[0]
+    row_out = both_out.at[pl.ds(0, block_rows), :]
+    col_out = both_out.at[pl.ds(block_rows, block_rows), :]
     p = lax.axis_index("tm")
     b = lax.axis_index("band")
     low = p < half
@@ -342,7 +343,6 @@
         line = source[pl.ds(index, 1), :]
         return pltpu.roll(jnp.broadcast_to(line, square), 1, 1, stride=1, stride_axis=0)
 
-    lane_quarter = lax.broadcasted_iota(jnp.int32, (LANES, quarter), 1)
 
     def build_rows():
         samples = rows_x[...]
@@ -368,25 +368,16 @@
             line = rows_back[pl.ds(index, 1), :]
             return pltpu.roll(jnp.broadcast_to(line, square), 0, 1, stride=1, stride_axis=0)
 
-        def column(which, index):
-            return jnp.sum(
-                jnp.where(lane_quarter == index, across[which], 0.0), axis=1, keepdims=True
-            )
-
-        turn0 = turned(0)
-        turn1 = turned(1)
-
-        def step(index, state):
-            turn, near = state
+        turn = turned(1)
+        near = jnp.where(keep, turned(0), turn)
+        for index in range(quarter):
             following = turned(index + 2)
             far = jnp.where(keep, turn, following)
-            c = column(0, index)
-            f = column(1, index)
+            c = across[0, :, index : index + 1]
+            f = across[1, :, index : index + 1]
             row_z[index, :, :LANES] = ((near - c) * f).astype(jnp.bfloat16)
             row_z[index, :, LANES:] = ((far - c) * f).astype(jnp.bfloat16)
-            return following, far
-
-        lax.fori_loop(0, quarter, step, (turn1, jnp.where(keep, turn0, turn1)), unroll=16)
+            turn, near = following, far
 
     starts = [starts_ref[c] for c in range(band_count)]
     whole = [lax.shift_right_logical(s, 7) for s in starts]
@@ -642,18 +633,19 @@
     blocks = lax.axis_size("tm")
     span = quarter + 8
     vmem = pl.BlockSpec(memory_space=pltpu.VMEM)
-    whole = jax.ShapeDtypeStruct((block_rows, LANES), jnp.float32)
+    length = series.shape[0]
+    outputs = jax.ShapeDtypeStruct((2 * block_rows, LANES), jnp.float32)
 
     operands = (band_starts, series.reshape(block_rows, LANES), tail.reshape(-1, LANES))
 
     def buffer(*shape, kind=jnp.float32):
         return pltpu.VMEM(shape, kind)
 
-    best_rows, best_cols = pl.pallas_call(
+    both = pl.pallas_call(
         functools.partial(pair_kernel, blocks),
-        out_shape=(whole, whole),
+        out_shape=outputs,
         in_specs=[pl.BlockSpec(memory_space=pltpu.HBM)] * 3,
-        out_specs=(vmem, vmem),
+        out_specs=vmem,
         scratch_shapes=[
             pltpu.SMEM((band_count,), jnp.int32),
             buffer(block_rows + span, LANES),
@@ -682,7 +674,8 @@
         ),
         name="banded_pairs",
     )(*[pltpu.with_memory_space_constraint(a, pltpu.HBM) for a in operands])
-    return best_rows.reshape(-1), best_cols.reshape(-1)
+    flat = both.reshape(-1)
+    return flat[:length], flat[length:]
 
 
 def solution(mesh):

time: 19.6 us -> 18.2 us (0.929)
  Pallas kernels: 17.5 us -> 16.7 us
  local copies, waits for them, and re-layouts: 1.27 us -> 0.66 us
    unnamed x2 -> x0, local copies, waits for them, and re-layouts: 1.27 us -> none
    pallas_call x1, Pallas kernels: 17.5 us -> 16.7 us  [spread_body(): pl.pallas_call(functools.partial(pair_kernel, blocks), out_shape=outputs,...]
    slice x0 -> x1, local copies, waits for them, and re-layouts: none -> 0.66 us  [spread_body(): return (flat[:length], flat[length:])]
where the time goes in v6:
time: 18.2 us; the launch traced here: 17.9 us
  Pallas kernels  16.7 us (92%)
  local copies, waits for them, and re-layouts  0.66 us (4%)
  between operations  0.64 us (4%)
    pallas_call x1, Pallas kernels, spread_body(): pl.pallas_call(functools.partial(pair_kernel, blocks), out_shape=outputs,...  16.7 us
    slice x1, local copies, waits for them, and re-layouts, spread_body(): return (flat[:length], flat[length:])  0.66 us

profile of v6, /device:TPU:0, one launch (start us, length us, event | category | flops | bytes accessed | tf_op | source)
XLA Modules:
  0.0 17.9 jit_solution(5793762131352677481)
XLA Ops:
  0.6 16.7 %banded_pairs.1 = f32[256,128]{1,0:T(8,128)S(1)} custom-call(s32[2]{0:T(128)} %starts_in.1, f32[128,128]{1,0:T(8,128)} %bitcast.6, f32[2,128]{1,0:T(2,128)} %bitcast.7), custom_call_target="tpu_custom_call" | custom-call | tf_op jit(solution)/shard_map/banded_pairs/pallas_call | solution.py:644
  17.3 0.7 %slice_bitcast_fusion = (f32[16384]{0:T(1024)}, f32[16384]{0:T(1024)}) fusion(f32[256,128]{1,0:T(8,128)S(1)} %banded_pairs.1), kind=kLoop, calls=%fused_computation | loop fusion | bytes 262144 | tf_op jit(solution)/shard_map/slice | solution.py:678

commit v7 on v6

--- a/solution.py
+++ b/solution.py
@@ -394,30 +394,31 @@
             stats[2 * c] = mean
             stats[2 * c + 1] = factor
 
-        def turned(c, index):
-            line = shifted[c, pl.ds(index, 1), :]
-            return pltpu.roll(jnp.broadcast_to(line, square), 1, 1, stride=1, stride_axis=0)
-
-        def one_band(c, _):
-            turn0 = turned(c, 0)
-            turn1 = turned(c, 1)
-
-            def step(index, state):
-                turn, near = state
-                following = turned(c, index + 2)
-                far = jnp.where(upper, turn, following)
-                center = stats[2 * c, pl.ds(index, 1), :]
-                factor = stats[2 * c + 1, pl.ds(index, 1), :]
-                col_z[c, index, :LANES, :] = ((near - center) * factor).astype(jnp.bfloat16)
-                col_z[c, index, LANES:, :] = ((far - center) * factor).astype(jnp.bfloat16)
-                return following, far
-
-            lax.fori_loop(
-                0, quarter + 1, step, (turn1, jnp.where(upper, turn0, turn1)), unroll=33
-            )
-            return 0
-
-        lax.fori_loop(0, band_count, one_band, 0)
+        for c in range(band_count - 1):
+            build_band(c)
+
+    def col_turned(c, index):
+        line = shifted[c, pl.ds(index, 1), :]
+        return pltpu.roll(jnp.broadcast_to(line, square), 1, 1, stride=1, stride_axis=0)
+
+    def col_begin(c):
+        turn = col_turned(c, 1)
+        return turn, jnp.where(upper, col_turned(c, 0), turn)
+
+    def col_tile(c, index, state):
+        turn, near = state
+        following = col_turned(c, index + 2)
+        far = jnp.where(upper, turn, following)
+        center = stats[2 * c, pl.ds(index, 1), :]
+        factor = stats[2 * c + 1, pl.ds(index, 1), :]
+        col_z[c, index, :LANES, :] = ((near - center) * factor).astype(jnp.bfloat16)
+        col_z[c, index, LANES:, :] = ((far - center) * factor).astype(jnp.bfloat16)
+        return following, far
+
+    def build_band(c):
+        state = col_begin(c)
+        for index in range(quarter + 1):
+            state = col_tile(c, index, state)
 
     def phase(turn, _):
         rows_now = lax.rem(turn + p // half, 2) == 0
@@ -475,9 +476,13 @@
         return tuple(left), rows_found
 
     floor = jnp.full((1, LANES), -1.0, jnp.float32)
-    pending, rows_found = lax.fori_loop(
-        0, quarter, score, ((floor,) * band_count, jnp.full(square, -1.0, jnp.float32)), unroll=16
-    )
+    ahead = band_count - 1
+    col_state = col_tile(ahead, 0, col_begin(ahead))
+    state = ((floor,) * band_count, jnp.full(square, -1.0, jnp.float32))
+    for index in range(quarter):
+        col_state = col_tile(ahead, index + 1, col_state)
+        state = score(index, state)
+    pending, rows_found = state
     row_res[...] = jnp.maximum(rows_found.T[:quarter], -1.0)
     lane_wide = lax.broadcasted_iota(jnp.int32, (2 * quarter, LANES), 1)
     reached = None

time: 18.2 us -> 20.9 us (1.15)
  Pallas kernels: 16.7 us -> 19.4 us
    pallas_call x1, Pallas kernels: 16.7 us -> 19.4 us  [spread_body(): pl.pallas_call(functools.partial(pair_kernel, blocks), out_shape=outputs,...]
where the time goes in v7:
time: 20.9 us; the launch traced here: 20.7 us
  Pallas kernels  19.4 us (93%)
  local copies, waits for them, and re-layouts  0.66 us (3%)
  between operations  0.64 us (3%)
    pallas_call x1, Pallas kernels, spread_body(): pl.pallas_call(functools.partial(pair_kernel, blocks), out_shape=outputs,...  19.4 us
    slice x1, local copies, waits for them, and re-layouts, spread_body(): return (flat[:length], flat[length:])  0.66 us

profile of v7, /device:TPU:0, one launch (start us, length us, event | category | flops | bytes accessed | tf_op | source)
XLA Modules:
  0.0 20.7 jit_solution(11133598941106761026)
XLA Ops:
  0.6 19.4 %banded_pairs.1 = f32[256,128]{1,0:T(8,128)S(1)} custom-call(s32[2]{0:T(128)} %starts_in.1, f32[128,128]{1,0:T(8,128)} %bitcast.6, f32[2,128]{1,0:T(2,128)} %bitcast.7), custom_call_target="tpu_custom_call" | custom-call | tf_op jit(solution)/shard_map/banded_pairs/pallas_call | solution.py:649
  20.1 0.7 %slice_bitcast_fusion = (f32[16384]{0:T(1024)}, f32[16384]{0:T(1024)}) fusion(f32[256,128]{1,0:T(8,128)S(1)} %banded_pairs.1), kind=kLoop, calls=%fused_computation | loop fusion | bytes 262144 | tf_op jit(solution)/shard_map/slice | solution.py:683

commit v8 on v6

--- a/solution.py
+++ b/solution.py
@@ -344,6 +344,11 @@
         return pltpu.roll(jnp.broadcast_to(line, square), 1, 1, stride=1, stride_axis=0)
 
 
+    def steps_of(line, begin):
+        few = pltpu.roll(jnp.broadcast_to(line, (8, LANES)), begin, 1, stride=1, stride_axis=0)
+        turns = [few] + [pltpu.roll(few, top, 1) for top in range(8, LANES, 8)]
+        return jnp.concatenate(turns, axis=0)
+
     def build_rows():
         samples = rows_x[...]
         mean, factor = moments_of(samples)
@@ -366,7 +371,7 @@
 
         def turned(index):
             line = rows_back[pl.ds(index, 1), :]
-            return pltpu.roll(jnp.broadcast_to(line, square), 0, 1, stride=1, stride_axis=0)
+            return steps_of(line, 0)
 
         turn = turned(1)
         near = jnp.where(keep, turned(0), turn)
@@ -396,7 +401,7 @@
 
         def turned(c, index):
             line = shifted[c, pl.ds(index, 1), :]
-            return pltpu.roll(jnp.broadcast_to(line, square), 1, 1, stride=1, stride_axis=0)
+            return steps_of(line, 1)
 
         def one_band(c, _):
             turn0 = turned(c, 0)
@@ -478,7 +483,6 @@
     pending, rows_found = lax.fori_loop(
         0, quarter, score, ((floor,) * band_count, jnp.full(square, -1.0, jnp.float32)), unroll=16
     )
-    row_res[...] = jnp.maximum(rows_found.T[:quarter], -1.0)
     lane_wide = lax.broadcasted_iota(jnp.int32, (2 * quarter, LANES), 1)
     reached = None
     for c in range(band_count):
@@ -523,6 +527,26 @@
     def _():
         slot_to[1].start()
         slot_to[2].start()
+
+    @pl.when(carry_sender)
+    def _():
+        carry_to[0].start()
+        carry_to[1].start()
+
+    @pl.when(jnp.logical_and(high, b == 0))
+    def _():
+        slot_to[0].start()
+        slots[2] = col_res[...]
+
+    @pl.when(jnp.logical_and(high, b == 1))
+    def _():
+        lower_to.start()
+        slots[3, lower, :] = col_res[lower, :]
+
+    row_res[...] = jnp.maximum(rows_found.T[:quarter], -1.0)
+
+    @pl.when(low)
+    def _():
         row_to[0].start()
         row_out[place, :] = row_res[...]
 
@@ -530,21 +554,6 @@
     def _():
         row_to[1].start()
         row_to[2].start()
-
-    @pl.when(jnp.logical_and(high, b == 0))
-    def _():
-        slot_to[0].start()
-        slots[2] = col_res[...]
-
-    @pl.when(carry_sender)
-    def _():
-        carry_to[0].start()
-        carry_to[1].start()
-
-    @pl.when(jnp.logical_and(high, b == 1))
-    def _():
-        lower_to.start()
-        slots[3, lower, :] = col_res[lower, :]
 
     def row_from(index):
         return remote(

time: 18.2 us -> 23.4 us (1.29)
  Pallas kernels: 16.7 us -> 21.9 us
    pallas_call x1, Pallas kernels: 16.7 us -> 21.9 us  [spread_body(): pl.pallas_call(functools.partial(pair_kernel, blocks), out_shape=outputs,...]
where the time goes in v8:
time: 23.4 us; the launch traced here: 23.2 us
  Pallas kernels  21.9 us (94%)
  local copies, waits for them, and re-layouts  0.66 us (3%)
  between operations  0.64 us (3%)
    pallas_call x1, Pallas kernels, spread_body(): pl.pallas_call(functools.partial(pair_kernel, blocks), out_shape=outputs,...  21.9 us
    slice x1, local copies, waits for them, and re-layouts, spread_body(): return (flat[:length], flat[length:])  0.66 us

profile of v8, /device:TPU:0, one launch (start us, length us, event | category | flops | bytes accessed | tf_op | source)
XLA Modules:
  0.0 23.2 jit_solution(4657532049886923519)
XLA Ops:
  0.6 21.9 %banded_pairs.1 = f32[256,128]{1,0:T(8,128)S(1)} custom-call(s32[2]{0:T(128)} %starts_in.1, f32[128,128]{1,0:T(8,128)} %bitcast.6, f32[2,128]{1,0:T(2,128)} %bitcast.7), custom_call_target="tpu_custom_call" | custom-call | tf_op jit(solution)/shard_map/banded_pairs/pallas_call | solution.py:653
  22.6 0.7 %slice_bitcast_fusion = (f32[16384]{0:T(1024)}, f32[16384]{0:T(1024)}) fusion(f32[256,128]{1,0:T(8,128)S(1)} %banded_pairs.1), kind=kLoop, calls=%fused_computation | loop fusion | bytes 262144 | tf_op jit(solution)/shard_map/slice | solution.py:687

commit v9 on v8

--- a/solution.py
+++ b/solution.py
@@ -344,16 +344,27 @@
         return pltpu.roll(jnp.broadcast_to(line, square), 1, 1, stride=1, stride_axis=0)
 
 
-    def steps_of(line, begin):
-        few = pltpu.roll(jnp.broadcast_to(line, (8, LANES)), begin, 1, stride=1, stride_axis=0)
-        turns = [few] + [pltpu.roll(few, top, 1) for top in range(8, LANES, 8)]
-        return jnp.concatenate(turns, axis=0)
-
     def build_rows():
         samples = rows_x[...]
         mean, factor = moments_of(samples)
-        across[0] = mean[:quarter].T
-        across[1] = factor[:quarter].T
+        for side, values in enumerate((mean[:quarter], factor[:quarter])):
+            left = values
+            pieces = []
+            for _ in range(3):
+                some = left.astype(jnp.bfloat16).astype(jnp.float32)
+                left = left - some
+                pieces.append(some)
+            pieces.append(jnp.zeros((LANES - 3 * quarter, LANES), jnp.float32))
+            turned_pieces = jnp.concatenate(pieces, axis=0).T.astype(jnp.bfloat16)
+            across[:, side * LANES : (side + 1) * LANES] = turned_pieces
+        wide = (2 * LANES, 2 * LANES)
+        ones = jnp.where(
+            (lax.broadcasted_iota(jnp.int32, wide, 0) < LANES)
+            == (lax.broadcasted_iota(jnp.int32, wide, 1) < LANES),
+            1.0,
+            0.0,
+        ).astype(jnp.bfloat16)
+        wide_lane = lax.rem(lax.broadcasted_iota(jnp.int32, (1, 2 * LANES), 1), quarter)
         flip = jnp.where(
             lax.broadcasted_iota(jnp.int32, square, 0) + lax.broadcasted_iota(jnp.int32, square, 1)
             == LANES - 1,
@@ -371,15 +382,17 @@
 
         def turned(index):
             line = rows_back[pl.ds(index, 1), :]
-            return steps_of(line, 0)
+            return pltpu.roll(jnp.broadcast_to(line, square), 0, 1, stride=1, stride_axis=0)
 
         turn = turned(1)
         near = jnp.where(keep, turned(0), turn)
         for index in range(quarter):
             following = turned(index + 2)
             far = jnp.where(keep, turn, following)
-            c = across[0, :, index : index + 1]
-            f = across[1, :, index : index + 1]
+            pick = jnp.where(wide_lane == index, 1.0, 0.0).astype(jnp.bfloat16)
+            spread = jnp.dot(across[...] * pick, ones, preferred_element_type=jnp.float32)
+            c = spread[:, :LANES]
+            f = spread[:, LANES:]
             row_z[index, :, :LANES] = ((near - c) * f).astype(jnp.bfloat16)
             row_z[index, :, LANES:] = ((far - c) * f).astype(jnp.bfloat16)
             turn, near = following, far
@@ -401,7 +414,7 @@
 
         def turned(c, index):
             line = shifted[c, pl.ds(index, 1), :]
-            return steps_of(line, 1)
+            return pltpu.roll(jnp.broadcast_to(line, square), 1, 1, stride=1, stride_axis=0)
 
         def one_band(c, _):
             turn0 = turned(c, 0)
@@ -662,7 +675,7 @@
             buffer(span, LANES),
             buffer(band_count, span, LANES),
             buffer(2 * band_count, span, LANES),
-            buffer(2, LANES, quarter),
+            buffer(LANES, 2 * LANES, kind=jnp.bfloat16),
             buffer(quarter, LANES, M, kind=jnp.bfloat16),
             buffer(band_count, quarter + 1, M, LANES, kind=jnp.bfloat16),
             buffer(band_count, 3 * quarter + 8, LANES),

time: 23.4 us -> 17.4 us (0.74)
  Pallas kernels: 21.9 us -> 15.9 us
    pallas_call x1, Pallas kernels: 21.9 us -> 15.9 us  [spread_body(): pl.pallas_call(functools.partial(pair_kernel, blocks), out_shape=outputs,...]
where the time goes in v9:
time: 17.4 us; the launch traced here: 17.2 us
  Pallas kernels  15.9 us (91%)
  local copies, waits for them, and re-layouts  0.66 us (4%)
  between operations  0.64 us (4%)
    pallas_call x1, Pallas kernels, spread_body(): pl.pallas_call(functools.partial(pair_kernel, blocks), out_shape=outputs,...  15.9 us
    slice x1, local copies, waits for them, and re-layouts, spread_body(): return (flat[:length], flat[length:])  0.66 us

profile of v9, /device:TPU:0, one launch (start us, length us, event | category | flops | bytes accessed | tf_op | source)
XLA Modules:
  0.0 17.2 jit_solution(14291589473270879562)
XLA Ops:
  0.6 15.9 %banded_pairs.1 = f32[256,128]{1,0:T(8,128)S(1)} custom-call(s32[2]{0:T(128)} %starts_in.1, f32[128,128]{1,0:T(8,128)} %bitcast.6, f32[2,128]{1,0:T(2,128)} %bitcast.7), custom_call_target="tpu_custom_call" | custom-call | tf_op jit(solution)/shard_map/banded_pairs/pallas_call | solution.py:666
  16.5 0.7 %slice_bitcast_fusion = (f32[16384]{0:T(1024)}, f32[16384]{0:T(1024)}) fusion(f32[256,128]{1,0:T(8,128)S(1)} %banded_pairs.1), kind=kLoop, calls=%fused_computation | loop fusion | bytes 262144 | tf_op jit(solution)/shard_map/slice | solution.py:700

commit v10 on v9

--- a/solution.py
+++ b/solution.py
@@ -494,7 +494,7 @@
 
     floor = jnp.full((1, LANES), -1.0, jnp.float32)
     pending, rows_found = lax.fori_loop(
-        0, quarter, score, ((floor,) * band_count, jnp.full(square, -1.0, jnp.float32)), unroll=16
+        0, quarter, score, ((floor,) * band_count, jnp.full(square, -1.0, jnp.float32)), unroll=32
     )
     lane_wide = lax.broadcasted_iota(jnp.int32, (2 * quarter, LANES), 1)
     reached = None

time: 17.4 us -> 17 us (0.977)
  Pallas kernels: 15.9 us -> 15.5 us
    pallas_call x1, Pallas kernels: 15.9 us -> 15.5 us  [spread_body(): pl.pallas_call(functools.partial(pair_kernel, blocks), out_shape=outputs,...]
where the time goes in v10:
time: 17 us; the launch traced here: 16.8 us
  Pallas kernels  15.5 us (91%)
  local copies, waits for them, and re-layouts  0.66 us (4%)
  between operations  0.64 us (4%)
    pallas_call x1, Pallas kernels, spread_body(): pl.pallas_call(functools.partial(pair_kernel, blocks), out_shape=outputs,...  15.5 us
    slice x1, local copies, waits for them, and re-layouts, spread_body(): return (flat[:length], flat[length:])  0.66 us

profile of v10, /device:TPU:0, one launch (start us, length us, event | category | flops | bytes accessed | tf_op | source)
XLA Modules:
  0.0 16.8 jit_solution(4275169915785339356)
XLA Ops:
  0.6 15.5 %banded_pairs.1 = f32[256,128]{1,0:T(8,128)S(1)} custom-call(s32[2]{0:T(128)} %starts_in.1, f32[128,128]{1,0:T(8,128)} %bitcast.6, f32[2,128]{1,0:T(2,128)} %bitcast.7), custom_call_target="tpu_custom_call" | custom-call | tf_op jit(solution)/shard_map/banded_pairs/pallas_call | solution.py:666
  16.1 0.7 %slice_bitcast_fusion = (f32[16384]{0:T(1024)}, f32[16384]{0:T(1024)}) fusion(f32[256,128]{1,0:T(8,128)S(1)} %banded_pairs.1), kind=kLoop, calls=%fused_computation | loop fusion | bytes 262144 | tf_op jit(solution)/shard_map/slice | solution.py:700
